TPU v7x, 32 devices: a whole 2x2x4 slice. The times are simulated.
32 devices in a mesh: vocab: 8 (over z, x), fsdp: 4 (over y, core).
Axes of the slice: x: 2, y: 2, z: 4, core: 2. Of those that a mesh axis runs over, the one named last changes fastest.
Arguments:
- hidden: bfloat16 [16384, 2048], P(('vocab', 'fsdp')), may hold values from -100 to 100
- head_weight: bfloat16 [262144, 2048], P(('vocab', 'fsdp')), may hold values from -2.5 to 2.5
- language_blocks: int32 [256, 6], replicated, may hold values from 0 to 7, as said below
- language_owner: int32 [256], replicated, may hold values from 0 to 255, each once
- token_language: int32 [16384, 1], P(('vocab', 'fsdp')), may hold values from 0 to 255; in each aligned block of 512 rows (0 to 511, 512 to 1023, ...) at most 4 rows name the same one
- labels: int32 [16384], P(('vocab', 'fsdp')), may hold values from 0 to 767
- loss_weight: bfloat16 [16384], P(('vocab', 'fsdp')), may hold values from 1 to 16
Outputs:
- hidden_grad: bfloat16 [16384, 2048], P(('vocab', 'fsdp'))
- token_loss: bfloat16 [16384], P(('vocab', 'fsdp'))
- head_grad: bfloat16 [262144, 2048], P(('vocab', 'fsdp'))
Inputs may be any that keep to these rules, and one draw needn't show every extreme that they name: `language_blocks`: each row names 6 different blocks. `language_owner`: each language slot is named by exactly one language. `token_language`: in each aligned group of 512 tokens no language is named more than 4 times, a bound that some block reaches in some or all groups.
All inputs are finite; a program needn't handle non-finite values.
Results may differ from a plain program's by a relative error of at most 0.0049.
Values may be sent and summed in bfloat16 or wider, within the bound.
A program may use at most 192 MiB of HBM per device.

v0:
```python
import jax
import jax.numpy as jnp
from jax import lax
from jax.sharding import PartitionSpec as P

D = 2048
BLOCK = 128
SB = 8
LB = 6
CAP = 4


SMOOTH = 0.1


def smoothed_loss(logits, targets, weights):
    columns = logits.shape[1]
    row_max = jnp.max(logits, axis=1, keepdims=True)
    shifted = logits - row_max
    log_probs = shifted - jnp.log(jnp.sum(jnp.exp(shifted), axis=1, keepdims=True))
    onehot = (lax.broadcasted_iota(jnp.int32, logits.shape, 1) == targets[:, None]).astype(
        jnp.float32
    )
    losses = -(1.0 - SMOOTH) * jnp.sum(onehot * log_probs, axis=1) - SMOOTH / columns * jnp.sum(
        log_probs, axis=1
    )
    grads = weights.astype(jnp.float32)[:, None] * (
        jnp.exp(log_probs) - (1.0 - SMOOTH) * onehot - SMOOTH / columns
    )
    return (losses.astype(jnp.bfloat16), grads.astype(jnp.bfloat16))


def slot_work(token_rows, weights, targets, slot_weights, blocks):
    candidates = jnp.take(slot_weights, blocks, axis=0).reshape(LB * BLOCK, D)
    logits = lax.dot_general(
        token_rows, candidates, (((1,), (1,)), ((), ())), preferred_element_type=jnp.float32
    )
    losses, grads = smoothed_loss(logits, targets, weights)
    row_grads = jnp.dot(grads, candidates, preferred_element_type=jnp.float32).astype(jnp.bfloat16)
    cand_grads = lax.dot_general(
        grads, token_rows, (((0,), (0,)), ((), ())), preferred_element_type=jnp.float32
    )
    slab_grads = (
        jnp.zeros((SB, BLOCK, D), jnp.float32).at[blocks].add(cand_grads.reshape(LB, BLOCK, D))
    )
    return (row_grads, losses, slab_grads.astype(jnp.bfloat16))


def place_tokens(token_language, language_owner):
    language = token_language[:, 0]
    languages = language_owner.shape[0]
    matches = language[:, None] == jnp.arange(languages, dtype=jnp.int32)[None, :]
    slot_ids = jnp.sum(jnp.where(matches, language_owner[None, :], 0), axis=1)
    positions = jnp.arange(language.shape[0], dtype=jnp.int32)
    earlier = (language[:, None] == language[None, :]) & (positions[None, :] < positions[:, None])
    rank_in_group = jnp.sum(earlier.astype(jnp.int32), axis=1)
    return slot_ids * CAP + rank_in_group


def by_slot(values, devices, owned_count):
    trailing = values.shape[3:]
    shaped = values.reshape((devices, owned_count, CAP) + trailing)
    return jnp.swapaxes(shaped, 0, 1).reshape((owned_count, devices * CAP) + trailing)


def to_grid(values, vocab_count, fsdp_count):
    owned_count = values.shape[0]
    trailing = values.shape[2:]
    shaped = values.reshape((owned_count, vocab_count * fsdp_count, CAP) + trailing)
    return jnp.swapaxes(shaped, 0, 1).reshape(
        (vocab_count, fsdp_count, owned_count * CAP) + trailing
    )


def shards(
    hidden, head_weight, language_blocks, language_owner, token_language, labels, loss_weight
):
    vocab_count = lax.axis_size("vocab")
    fsdp_count = lax.axis_size("fsdp")
    devices = vocab_count * fsdp_count
    languages = language_owner.shape[0]
    owned_count = languages // devices
    places = languages * CAP
    features = hidden.shape[1]
    target_place = place_tokens(token_language, language_owner)
    send_rows = jnp.zeros((places, features), jnp.bfloat16).at[target_place].set(hidden)
    send_weights = jnp.zeros((places,), jnp.bfloat16).at[target_place].set(loss_weight)
    send_labels = jnp.zeros((places,), jnp.int32).at[target_place].set(labels)
    grid_shape = (vocab_count, fsdp_count, owned_count * CAP)
    outgoing = (
        send_rows.reshape(grid_shape + (features,)),
        send_weights.reshape(grid_shape),
        send_labels.reshape(grid_shape),
    )
    incoming = (
        lax.all_to_all(
            lax.all_to_all(outgoing[0], "vocab", split_axis=0, concat_axis=0, tiled=True),
            "fsdp",
            split_axis=1,
            concat_axis=1,
            tiled=True,
        ),
        lax.all_to_all(
            lax.all_to_all(outgoing[1], "vocab", split_axis=0, concat_axis=0, tiled=True),
            "fsdp",
            split_axis=1,
            concat_axis=1,
            tiled=True,
        ),
        lax.all_to_all(
            lax.all_to_all(outgoing[2], "vocab", split_axis=0, concat_axis=0, tiled=True),
            "fsdp",
            split_axis=1,
            concat_axis=1,
            tiled=True,
        ),
    )
    self_index = lax.axis_index(("vocab", "fsdp"))
    slot_inputs = (
        jnp.arange(owned_count, dtype=jnp.int32),
        by_slot(incoming[0], devices, owned_count),
        by_slot(incoming[1], devices, owned_count),
        by_slot(incoming[2], devices, owned_count),
        head_weight.reshape(owned_count, SB, BLOCK, features),
    )

    def one_slot(slot_items):
        slot_local, token_rows, weights, targets, slot_weights = slot_items
        owned_mask = (language_owner == self_index * owned_count + slot_local).astype(jnp.int32)
        blocks = jnp.sum(owned_mask[:, None] * language_blocks, axis=0)
        return slot_work(token_rows, weights, targets, slot_weights, blocks)

    row_grads, losses, slab_grads = lax.map(one_slot, slot_inputs)
    returning = (
        to_grid(row_grads, vocab_count, fsdp_count),
        to_grid(losses, vocab_count, fsdp_count),
    )
    returned = (
        lax.all_to_all(
            lax.all_to_all(returning[0], "vocab", split_axis=0, concat_axis=0, tiled=True),
            "fsdp",
            split_axis=1,
            concat_axis=1,
            tiled=True,
        ),
        lax.all_to_all(
            lax.all_to_all(returning[1], "vocab", split_axis=0, concat_axis=0, tiled=True),
            "fsdp",
            split_axis=1,
            concat_axis=1,
            tiled=True,
        ),
    )
    returned_rows = returned[0].reshape(places, features)
    returned_loss = returned[1].reshape(places)
    hidden_grad = jnp.take(returned_rows, target_place, axis=0)
    token_loss = jnp.take(returned_loss, target_place, axis=0)
    return (hidden_grad, token_loss, slab_grads.reshape(owned_count * SB * BLOCK, features))


def solution(mesh):
    in_specs = (
        P(("vocab", "fsdp"), None),
        P(("vocab", "fsdp"), None),
        P(),
        P(),
        P(("vocab", "fsdp"), None),
        P(("vocab", "fsdp")),
        P(("vocab", "fsdp")),
    )
    out_specs = (P(("vocab", "fsdp"), None), P(("vocab", "fsdp")), P(("vocab", "fsdp"), None))
    return jax.shard_map(shards, mesh=mesh, in_specs=in_specs, out_specs=out_specs, check_vma=False)
```

profile of v0, /device:TPU:0, one launch (start us, length us, event | category | flops | bytes accessed | tf_op | source)
XLA Modules:
  0.0 764.9 jit_solution(17435921190379290526)
XLA Ops:
  6.6 13.6 %all_to_all.50 = bf16[8,4,32]{2,1,0:T(4,128)(2,1)S(1)} all-to-all(bf16[8,4,32]{2,1,0:T(4,128)(2,1)S(1)} %reshape.214), channel_id=1, replica_groups=mesh['vocab'=8,'fsdp'=4] {'vocab'}, dimensions={0} | all-to-all | bytes 4096 | tf_op jit(solution)/shard_map/all_to_all | solution.py:104
  31.0 7.3 scatter_custom_fusion.2
  38.3 5.9 all-to-all-start.2
  46.1 91.5 %all-to-all-done.2 = bf16[8,4,32,2048]{3,2,1,0:T(8,128)(2,1)} async-done(((bf16[8,4,32,2048]{3,2,1,0:T(8,128)(2,1)}), bf16[8,4,32,2048]{3,2,1,0:T(8,128)(2,1)}, u32[]{:S(2)}, u32[]{:S(2)}) %all-to-all-start.2) | async-done | bytes 4194336 | tf_op jit(solution)/shard_map/all_to_all | solution.py:97
  152.4 46.5 %all-to-all-done.3 = bf16[8,4,32,2048]{3,2,0,1:T(8,128)(2,1)} async-done(((bf16[8,4,32,2048]{3,2,0,1:T(8,128)(2,1)}), bf16[8,4,32,2048]{3,2,0,1:T(8,128)(2,1)}, u32[]{:S(2)}, u32[]{:S(2)}) %all-to-all-start.3) | async-done | bytes 4194336 | tf_op jit(solution)/shard_map/all_to_all | solution.py:96
  203.6 7.2 reshape.218
  210.8 6.6 copy.91
  221.7 344.1 %while.16 = (s32[]{:T(128)}, bf16[8,128,2048]{2,1,0:T(8,128)(2,1)}, bf16[8,128]{1,0:T(8,128)(2,1)S(1)}, bf16[8,8,128,2048]{3,2,1,0:T(8,128)(2,1)}, bf16[8,128]{1...) while((s32[]{:T(128)}, bf16[8,128,2048]{2,1,0:T(8,128)(2,1)}, ...), condition=%wide.region_12.13_spmd, body=%wide.region_5.12_spmd.sunk | while | flops 1217499904 | bytes 84045200 | solution.py:133
  245.4 13.2 %scatter_fusion = f32[8,128,2048]{2,1,0:T(8,128)} fusion(f32[8,128,2048]{2,1,0:T(8,128)} %broadcast.283, s32[6]{0:T(128)S(1)} %fusion.54, f32[6,128,2048]{2,1,0:T(8,128)} %fusion.60), kind=kCustom, calls=%fused_computation.3.clone.1 | custom fusion | flops 1572864 | bytes 18874392 | tf_op jit(solution)/shard_map/while/body/eval_jaxpr/scatter-add | solution.py:44
  258.6 6.0 bitcast_dynamic-update-slice_fusion.2
  288.4 13.2 %scatter_fusion = f32[8,128,2048]{2,1,0:T(8,128)} fusion(f32[8,128,2048]{2,1,0:T(8,128)} %broadcast.283, s32[6]{0:T(128)S(1)} %fusion.54, f32[6,128,2048]{2,1,0:T(8,128)} %fusion.60), kind=kCustom, calls=%fused_computation.3.clone.1 | custom fusion | flops 1572864 | bytes 18874392 | tf_op jit(solution)/shard_map/while/body/eval_jaxpr/scatter-add | solution.py:44
  301.6 6.0 bitcast_dynamic-update-slice_fusion.2
  331.4 13.2 %scatter_fusion = f32[8,128,2048]{2,1,0:T(8,128)} fusion(f32[8,128,2048]{2,1,0:T(8,128)} %broadcast.283, s32[6]{0:T(128)S(1)} %fusion.54, f32[6,128,2048]{2,1,0:T(8,128)} %fusion.60), kind=kCustom, calls=%fused_computation.3.clone.1 | custom fusion | flops 1572864 | bytes 18874392 | tf_op jit(solution)/shard_map/while/body/eval_jaxpr/scatter-add | solution.py:44
  344.6 6.0 bitcast_dynamic-update-slice_fusion.2
  374.4 13.2 %scatter_fusion = f32[8,128,2048]{2,1,0:T(8,128)} fusion(f32[8,128,2048]{2,1,0:T(8,128)} %broadcast.283, s32[6]{0:T(128)S(1)} %fusion.54, f32[6,128,2048]{2,1,0:T(8,128)} %fusion.60), kind=kCustom, calls=%fused_computation.3.clone.1 | custom fusion | flops 1572864 | bytes 18874392 | tf_op jit(solution)/shard_map/while/body/eval_jaxpr/scatter-add | solution.py:44
  387.6 6.0 bitcast_dynamic-update-slice_fusion.2
  417.4 13.3 %scatter_fusion = f32[8,128,2048]{2,1,0:T(8,128)} fusion(f32[8,128,2048]{2,1,0:T(8,128)} %broadcast.283, s32[6]{0:T(128)S(1)} %fusion.54, f32[6,128,2048]{2,1,0:T(8,128)} %fusion.60), kind=kCustom, calls=%fused_computation.3.clone.1 | custom fusion | flops 1572864 | bytes 18874392 | tf_op jit(solution)/shard_map/while/body/eval_jaxpr/scatter-add | solution.py:44
  430.7 6.0 bitcast_dynamic-update-slice_fusion.2
  460.5 13.2 %scatter_fusion = f32[8,128,2048]{2,1,0:T(8,128)} fusion(f32[8,128,2048]{2,1,0:T(8,128)} %broadcast.283, s32[6]{0:T(128)S(1)} %fusion.54, f32[6,128,2048]{2,1,0:T(8,128)} %fusion.60), kind=kCustom, calls=%fused_computation.3.clone.1 | custom fusion | flops 1572864 | bytes 18874392 | tf_op jit(solution)/shard_map/while/body/eval_jaxpr/scatter-add | solution.py:44
  473.7 6.0 bitcast_dynamic-update-slice_fusion.2
  503.5 13.2 %scatter_fusion = f32[8,128,2048]{2,1,0:T(8,128)} fusion(f32[8,128,2048]{2,1,0:T(8,128)} %broadcast.283, s32[6]{0:T(128)S(1)} %fusion.54, f32[6,128,2048]{2,1,0:T(8,128)} %fusion.60), kind=kCustom, calls=%fused_computation.3.clone.1 | custom fusion | flops 1572864 | bytes 18874392 | tf_op jit(solution)/shard_map/while/body/eval_jaxpr/scatter-add | solution.py:44
  516.6 6.0 bitcast_dynamic-update-slice_fusion.2
  546.4 13.3 %scatter_fusion = f32[8,128,2048]{2,1,0:T(8,128)} fusion(f32[8,128,2048]{2,1,0:T(8,128)} %broadcast.283, s32[6]{0:T(128)S(1)} %fusion.54, f32[6,128,2048]{2,1,0:T(8,128)} %fusion.60), kind=kCustom, calls=%fused_computation.3.clone.1 | custom fusion | flops 1572864 | bytes 18874392 | tf_op jit(solution)/shard_map/while/body/eval_jaxpr/scatter-add | solution.py:44
  559.7 6.0 bitcast_dynamic-update-slice_fusion.2
  570.8 7.2 reshape.224
  578.0 7.1 copy.109
  585.1 6.9 reshape.225
  592.0 6.0 all-to-all-start.6
  598.7 91.5 %all-to-all-done.6 = bf16[8,4,32,2048]{3,2,1,0:T(8,128)(2,1)} async-done(((bf16[8,4,32,2048]{3,2,1,0:T(8,128)(2,1)}), bf16[8,4,32,2048]{3,2,1,0:T(8,128)(2,1)}, u32[]{:S(2)}, u32[]{:S(2)}) %all-to-all-start.6) | async-done | bytes 4194336 | tf_op jit(solution)/shard_map/all_to_all | solution.py:140
  698.2 5.1 all-to-all-start.7
  707.6 43.9 %all-to-all-done.7 = bf16[8,4,32,2048]{3,2,0,1:T(8,128)(2,1)} async-done(((bf16[8,4,32,2048]{3,2,0,1:T(8,128)(2,1)}), bf16[8,4,32,2048]{3,2,0,1:T(8,128)(2,1)}, u32[]{:S(2)}, u32[]{:S(2)}) %all-to-all-start.7) | async-done | bytes 4194336 | tf_op jit(solution)/shard_map/all_to_all | solution.py:139
  756.2 7.1 gather_fusion.1
  (255 shorter events, 250.8 us)
Async XLA Ops:
  20.8 6.9 all-to-all-start.1
  27.7 10.6 %all-to-all-start.4 = ((s32[8,1,128]{2,1,0:T(1,128)}), s32[8,1,128]{2,1,0:T(1,128)S(1)}, u32[]{:S(2)}, u32[]{:S(2)}) async-start(s32[8,1,128]{2,1,0:T(1,128)} %reshape.297), calls=%async_computation.4 | async-start | bytes 8192 | tf_op jit(solution)/shard_map/all_to_all | solution.py:111
  38.3 99.3 %all-to-all-start.2 = ((bf16[8,4,32,2048]{3,2,1,0:T(8,128)(2,1)}), bf16[8,4,32,2048]{3,2,1,0:T(8,128)(2,1)}, u32[]{:S(2)}, u32[]{:S(2)}) async-start(bf16[8,4,32,2048]{3,2,1,0:T(8,128)(2,1)} %bitcast.121), calls=%async_computation.2 | async-start | bytes 8388608 | tf_op jit(solution)/shard_map/all_to_all | solution.py:97
  137.6 8.0 %all-to-all-start.5 = ((s32[4,1,256]{2,1,0:T(1,128)}), s32[4,1,256]{2,1,0:T(1,128)S(1)}, u32[]{:S(2)}, u32[]{:S(2)}) async-start(s32[4,1,256]{2,1,0:T(1,128)} %reshape.299), calls=%async_computation.5 | async-start | bytes 8192 | tf_op jit(solution)/shard_map/all_to_all | solution.py:110
  145.6 53.2 %all-to-all-start.3 = ((bf16[8,4,32,2048]{3,2,0,1:T(8,128)(2,1)}), bf16[8,4,32,2048]{3,2,0,1:T(8,128)(2,1)}, u32[]{:S(2)}, u32[]{:S(2)}) async-start(bf16[8,4,32,2048]{3,2,0,1:T(8,128)(2,1)} %copy.89), calls=%async_computation.3 | async-start | bytes 8388608 | tf_op jit(solution)/shard_map/all_to_all | solution.py:96
  217.4 4.3 copy-start
  217.4 4.3 copy-start.1
  566.9 25.1 %all-to-all-start.8 = ((bf16[8,4,32]{2,1,0:T(4,128)(2,1)}), bf16[8,4,32]{2,1,0:T(4,128)(2,1)S(1)}, u32[]{:S(2)}, u32[]{:S(2)}) async-start(bf16[8,4,32]{2,1,0:T(4,128)(2,1)} %reshape.228), calls=%async_computation.8 | async-start | bytes 16384 | tf_op jit(solution)/shard_map/all_to_all | solution.py:147
  592.0 98.2 %all-to-all-start.6 = ((bf16[8,4,32,2048]{3,2,1,0:T(8,128)(2,1)}), bf16[8,4,32,2048]{3,2,1,0:T(8,128)(2,1)}, u32[]{:S(2)}, u32[]{:S(2)}) async-start(bf16[8,4,32,2048]{3,2,1,0:T(8,128)(2,1)} %reshape.225), calls=%async_computation.6 | async-start | bytes 8388608 | tf_op jit(solution)/shard_map/all_to_all | solution.py:140
  690.2 8.0 %all-to-all-start.9 = ((bf16[4,2,128]{2,1,0:T(2,128)(2,1)}), bf16[4,2,128]{2,1,0:T(2,128)(2,1)S(1)}, u32[]{:S(2)}, u32[]{:S(2)}) async-start(bf16[4,2,128]{2,1,0:T(2,128)(2,1)} %reshape.301), calls=%async_computation.9 | async-start | bytes 4096 | tf_op jit(solution)/shard_map/all_to_all | solution.py:146
  698.2 53.3 %all-to-all-start.7 = ((bf16[8,4,32,2048]{3,2,0,1:T(8,128)(2,1)}), bf16[8,4,32,2048]{3,2,0,1:T(8,128)(2,1)}, u32[]{:S(2)}, u32[]{:S(2)}) async-start(bf16[8,4,32,2048]{3,2,0,1:T(8,128)(2,1)} %copy.99), calls=%async_computation.7 | async-start | bytes 8388608 | tf_op jit(solution)/shard_map/all_to_all | solution.py:139
where the time goes:
time: 768 us; the launch traced here: 765 us
  waiting for transfers between devices  274 us (36%)
  local copies, waits for them, and re-layouts  191 us (25%)
  other arithmetic  173 us (23%)
  matrix products  68.3 us (9%)
  starting transfers between devices  39 us (5%)
  blocking collectives  13.6 us (2%)
    scatter-add x8, other arithmetic, slot_work(): jnp.zeros((SB, BLOCK, D), jnp.float32).at[blocks]  106 us
    all_to_all x1, waiting for transfers between devices, shards(): lax.all_to_all(outgoing[0], 'vocab', split_axis=0, concat_axis=0, tiled=T...  91.5 us
    all_to_all x1, waiting for transfers between devices, shards(): lax.all_to_all(returning[0], 'vocab', split_axis=0, concat_axis=0, tiled=...  91.5 us
    dynamic_update_slice x8, other arithmetic, shards(): row_grads, losses, slab_grads = lax.map(one_slot, slot_inputs)  48.4 us
    all_to_all x1, waiting for transfers between devices, shards(): lax.all_to_all(lax.all_to_all(outgoing[0], 'vocab', split_axis=0, concat_...  46.5 us
    all_to_all x1, waiting for transfers between devices, shards(): lax.all_to_all(lax.all_to_all(returning[0], 'vocab', split_axis=0, concat...  43.9 us
    dot_general x8, matrix products, slot_work(): lax.dot_general(grads, token_rows, (((0,), (0,)), ((), ())), preferred_el...  37.8 us
    squeeze x8, local copies, waits for them, and re-layouts, shards(): row_grads, losses, slab_grads = lax.map(one_slot, slot_inputs)  37.6 us
  transfers between devices with their start and end apart: 9, of which 5 were waited for; matrix products, arithmetic and copies ran while one was open for 7% of the time, Pallas kernels for 0%

commit v1 on v0

v1 whole, which is shorter than its diff:
```python
import functools

import jax
import jax.numpy as jnp
from jax import lax
from jax.experimental import pallas as pl
from jax.experimental.pallas import tpu as pltpu
from jax.sharding import PartitionSpec as P

BLOCK = 128
SB = 8
LB = 6
CAP = 4
SMOOTH = 0.1
AXES = ("vocab", "fsdp")
EXTRA = 128
VMEM = 56 * 1024 * 1024


def one_hot(condition):
    return condition.astype(jnp.float32).astype(jnp.bfloat16)


def placing(place_row, chunk, chunks, per, rows):
    index = lax.broadcasted_iota(jnp.int32, (rows, 1), 0)
    place = (index // per) * (per * chunks) + chunk * per + index % per
    return one_hot(place == place_row)


def dispatch_kernel(chunks, per, lang_col, lang_row, owner_col, hidden, meta, place_out, *outs):
    tokens = hidden.shape[0]
    languages = owner_col.shape[0]
    language_ids = lax.broadcasted_iota(jnp.int32, (languages, tokens), 0)
    slot = jnp.sum(
        jnp.where(language_ids == lang_row[...], owner_col[...], 0), axis=0, keepdims=True
    )
    before = lax.broadcasted_iota(jnp.int32, (tokens, tokens), 0) < lax.broadcasted_iota(
        jnp.int32, (tokens, tokens), 1
    )
    same = lang_col[...] == lang_row[...]
    rank = jnp.sum(jnp.where(same & before, 1, 0), axis=0, keepdims=True)
    place = slot * CAP + rank
    place_out[...] = place
    features = hidden.shape[1]
    for chunk, out in enumerate(outs):
        picks = placing(place, chunk, chunks, per, out.shape[0])
        out[:, :features] = jnp.dot(
            picks, hidden[...], preferred_element_type=jnp.float32
        ).astype(jnp.bfloat16)
        out[:, features:] = jnp.dot(
            picks, meta[...], preferred_element_type=jnp.float32
        ).astype(jnp.bfloat16)


def slots_kernel(slots, first, blocks, incoming, slab, back, rows_out, grads_out, held):
    step = pl.program_id(0)
    total = incoming.shape[0]
    rows = total // slots
    features = slab.shape[1]
    columns = slab.shape[0]
    per = CAP * slots
    if slots > 1:
        wanted = lax.broadcasted_iota(jnp.int32, (rows, 1), 0)
        wanted = (wanted // CAP) * per + step * CAP + wanted % CAP
        picks = one_hot(wanted == lax.broadcasted_iota(jnp.int32, (rows, total), 1))
        rows_out[...] = jnp.dot(
            picks, incoming[:, :features], preferred_element_type=jnp.float32
        ).astype(jnp.bfloat16)
        extra = jnp.dot(picks, incoming[:, features:], preferred_element_type=jnp.float32)
    else:
        rows_out[...] = incoming[:, :features]
        extra = incoming[:, features:].astype(jnp.float32)
    weights = extra[:, 0:1]
    targets = (extra[:, 1:2] * BLOCK + extra[:, 2:3]).astype(jnp.int32)
    column = lax.broadcasted_iota(jnp.int32, (1, columns), 1)
    listed = jnp.full((1, columns), -1, jnp.int32)
    for j in range(LB):
        named = blocks[(first + step) * LB + j]
        listed = jnp.where(column // BLOCK == named, j * BLOCK + column % BLOCK, listed)
    used = listed >= 0
    logits = lax.dot_general(
        rows_out[...], slab[...], (((1,), (1,)), ((), ())), preferred_element_type=jnp.float32
    )
    count = LB * BLOCK
    row_max = jnp.max(jnp.where(used, logits, -jnp.inf), axis=1, keepdims=True)
    shifted = jnp.where(used, logits - row_max, 0.0)
    powers = jnp.where(used, jnp.exp(shifted), 0.0)
    sums = jnp.sum(powers, axis=1, keepdims=True)
    log_sums = jnp.log(sums)
    is_target = listed == targets
    at_target = jnp.sum(jnp.where(is_target, shifted, 0.0), axis=1, keepdims=True) - log_sums
    all_of_them = jnp.sum(shifted, axis=1, keepdims=True) - count * log_sums
    losses = -(1.0 - SMOOTH) * at_target - SMOOTH / count * all_of_them
    grads = weights * (
        powers * (1.0 / sums) - jnp.where(is_target, 1.0 - SMOOTH, 0.0) - SMOOTH / count
    )
    grads = jnp.where(used, grads, 0.0).astype(jnp.bfloat16)
    grads_out[...] = grads
    row_grads = jnp.dot(grads, slab[...], preferred_element_type=jnp.float32).astype(jnp.bfloat16)
    lane = lax.broadcasted_iota(jnp.int32, (rows, EXTRA), 1)
    tail = jnp.where(lane == 0, losses, 0.0).astype(jnp.bfloat16)
    if slots > 1:
        here = pl.ds(pl.multiple_of(step * rows, rows), rows)
        held[here, :features] = row_grads
        held[here, features:] = tail

        @pl.when(step == slots - 1)
        def _():
            index = lax.broadcasted_iota(jnp.int32, (total, 1), 0)
            source = ((index % per) // CAP) * rows + (index // per) * CAP + index % CAP
            spread = one_hot(source == lax.broadcasted_iota(jnp.int32, (total, total), 1))
            back[...] = jnp.dot(spread, held[...], preferred_element_type=jnp.float32).astype(
                jnp.bfloat16
            )
    else:
        back[:, :features] = row_grads
        back[:, features:] = tail


def head_kernel(chunks, slots, *refs):
    out = refs[-1]
    step = pl.program_id(0)
    for chunk in range(chunks):
        rows, grads = refs[2 * chunk], refs[2 * chunk + 1]

        @pl.when(step // slots == chunk)
        def _():
            out[...] = lax.dot_general(
                grads[...], rows[...], (((0,), (0,)), ((), ())),
                preferred_element_type=jnp.float32,
            ).astype(jnp.bfloat16)


def combine_kernel(chunks, per, place, *refs):
    returned, (hidden_out, loss_out) = refs[:chunks], refs[chunks:]
    features = hidden_out.shape[1]
    total, losses = None, None
    for chunk, part in enumerate(returned):
        picks = placing(place[...], chunk, chunks, per, part.shape[0])
        rows = lax.dot_general(
            picks, part[:, :features], (((0,), (0,)), ((), ())),
            preferred_element_type=jnp.float32,
        )
        loss = lax.dot_general(
            part[:, features:], picks, (((0,), (0,)), ((), ())),
            preferred_element_type=jnp.float32,
        )
        total = rows if total is None else total + rows
        losses = loss if losses is None else losses + loss
    hidden_out[...] = total.astype(jnp.bfloat16)
    loss_out[...] = losses[0:1, :].astype(jnp.bfloat16)


def shards(
    hidden, head_weight, language_blocks, language_owner, token_language, labels, loss_weight
):
    devices = lax.axis_size("vocab") * lax.axis_size("fsdp")
    languages = language_owner.shape[0]
    tokens, features = hidden.shape
    owned = languages // devices
    chunks = 2 if owned % 2 == 0 else 1
    slots = owned // chunks
    per = slots * CAP
    chunk_rows = devices * per
    slot_rows = devices * CAP
    slab_rows = SB * BLOCK
    width = features + EXTRA
    params = pltpu.CompilerParams(vmem_limit_bytes=VMEM)

    lane = lax.broadcasted_iota(jnp.int32, (tokens, EXTRA), 1)
    label_col = labels[:, None]
    parts = jnp.where(lane == 1, label_col // BLOCK, label_col % BLOCK)
    meta = jnp.where(
        lane == 0, loss_weight[:, None].astype(jnp.float32), parts.astype(jnp.float32)
    )
    meta = jnp.where(lane < 3, meta, 0.0).astype(jnp.bfloat16)
    place, *outgoing = pl.pallas_call(
        functools.partial(dispatch_kernel, chunks, per),
        out_shape=[jax.ShapeDtypeStruct((1, tokens), jnp.int32)]
        + [jax.ShapeDtypeStruct((chunk_rows, width), jnp.bfloat16)] * chunks,
        compiler_params=params,
        cost_estimate=pl.CostEstimate(
            flops=2 * chunks * chunk_rows * tokens * width, bytes_accessed=8 << 20, transcendentals=0
        ),
    )(token_language, token_language.reshape(1, tokens), language_owner[:, None], hidden, meta)

    self_index = lax.axis_index(AXES)
    own_slots = self_index * owned + jnp.arange(owned, dtype=jnp.int32)
    owns = (own_slots[:, None] == language_owner[None, :]).astype(jnp.int32)
    blocks = jnp.sum(owns[:, :, None] * language_blocks[None], axis=1).reshape(-1)

    def exchange(values):
        shaped = values.reshape(devices, per, width)
        return lax.all_to_all(shaped, AXES, split_axis=0, concat_axis=0, tiled=True).reshape(
            chunk_rows, width
        )

    incoming = [exchange(values) for values in outgoing]
    kept, returned = [], []
    for chunk in range(chunks):
        first = chunk * slots
        back, rows, grads = pl.pallas_call(
            functools.partial(slots_kernel, slots, first),
            out_shape=[
                jax.ShapeDtypeStruct((chunk_rows, width), jnp.bfloat16),
                jax.ShapeDtypeStruct((slots * slot_rows, features), jnp.bfloat16),
                jax.ShapeDtypeStruct((slots * slot_rows, slab_rows), jnp.bfloat16),
            ],
            grid_spec=pltpu.PrefetchScalarGridSpec(
                num_scalar_prefetch=1,
                grid=(slots,),
                in_specs=[
                    pl.BlockSpec((chunk_rows, width), lambda s, b: (0, 0)),
                    pl.BlockSpec((slab_rows, features), lambda s, b, first=first: (first + s, 0)),
                ],
                out_specs=[
                    pl.BlockSpec((chunk_rows, width), lambda s, b: (0, 0)),
                    pl.BlockSpec((slot_rows, features), lambda s, b: (s, 0)),
                    pl.BlockSpec((slot_rows, slab_rows), lambda s, b: (s, 0)),
                ],
                scratch_shapes=[pltpu.VMEM((chunk_rows, width), jnp.bfloat16)],
            ),
            compiler_params=params,
            cost_estimate=pl.CostEstimate(
                flops=4 * slots * slot_rows * slab_rows * features,
                bytes_accessed=2 * slots * slab_rows * features + (12 << 20),
                transcendentals=0,
            ),
        )(blocks, incoming[chunk], head_weight)
        kept += [rows, grads]
        returned.append(exchange(back))

    kept_specs = []
    for chunk in range(chunks):

        def at(s, chunk=chunk):
            return (jnp.clip(s - chunk * slots, 0, slots - 1), 0)

        kept_specs += [
            pl.BlockSpec((slot_rows, features), at),
            pl.BlockSpec((slot_rows, slab_rows), at),
        ]
    head_grad = pl.pallas_call(
        functools.partial(head_kernel, chunks, slots),
        out_shape=jax.ShapeDtypeStruct(head_weight.shape, jnp.bfloat16),
        grid=(owned,),
        in_specs=kept_specs,
        out_specs=pl.BlockSpec((slab_rows, features), lambda s: (s, 0)),
        compiler_params=params,
        cost_estimate=pl.CostEstimate(
            flops=2 * owned * slot_rows * slab_rows * features,
            bytes_accessed=2 * owned * slab_rows * features,
            transcendentals=0,
        ),
    )(*kept)
    hidden_grad, token_loss = pl.pallas_call(
        functools.partial(combine_kernel, chunks, per),
        out_shape=[
            jax.ShapeDtypeStruct((tokens, features), jnp.bfloat16),
            jax.ShapeDtypeStruct((1, tokens), jnp.bfloat16),
        ],
        compiler_params=params,
        cost_estimate=pl.CostEstimate(
            flops=2 * chunks * chunk_rows * tokens * width, bytes_accessed=8 << 20, transcendentals=0
        ),
    )(place, *returned)
    return hidden_grad, token_loss.reshape(tokens), head_grad


def solution(mesh):
    in_specs = (
        P(AXES, None),
        P(AXES, None),
        P(),
        P(),
        P(AXES, None),
        P(AXES),
        P(AXES),
    )
    out_specs = (P(AXES, None), P(AXES), P(AXES, None))
    return jax.shard_map(shards, mesh=mesh, in_specs=in_specs, out_specs=out_specs, check_vma=False)
```

time: 768 us -> 249 us (0.32)
  local copies, waits for them, and re-layouts: 191 us -> 6.39 us
  waiting for transfers between devices: 274 us -> 101 us
  other arithmetic: 173 us -> 3.79 us
  matrix products: 68.3 us -> 0 us
  Pallas kernels: 0 us -> 64.7 us
  blocking collectives: 13.6 us -> 60.5 us
  starting transfers between devices: 39 us -> 11.4 us
    all_to_all x9 -> x3, waiting for transfers between devices: 274 us -> 101 us  [exchange(): lax.all_to_all(shaped, AXES, split_axis=0, concat_axis=0, tiled=True)]
    scatter-add x8 -> x0, other arithmetic: 106 us -> none  [slot_work(): jnp.zeros((SB, BLOCK, D), jnp.float32).at[blocks]]
    dot_general x24 -> x0, matrix products: 68.3 us -> none  [the longest x8 37.8 us: slot_work(): lax.dot_general(grads, token_rows, (((0,), (0,)), ((), ())), preferred_el...]
    pallas_call x0 -> x5, Pallas kernels: none -> 64.7 us  [the longest x2 36.4 us: shards(): pl.pallas_call(functools.partial(slots_kernel, slots, first), out_shape=[...]
    dynamic_update_slice x8 -> x0, other arithmetic: 48.4 us -> none  [shards(): row_grads, losses, slab_grads = lax.map(one_slot, slot_inputs)]
    all_to_all x1, blocking collectives: 13.6 us -> 60.5 us  [exchange(): lax.all_to_all(shaped, AXES, split_axis=0, concat_axis=0, tiled=True)]
    squeeze x8 -> x0, local copies, waits for them, and re-layouts: 37.6 us -> none  [shards(): row_grads, losses, slab_grads = lax.map(one_slot, slot_inputs)]
    another operation x8 -> x0, local copies, waits for them, and re-layouts: 34.2 us -> none
  transfers between devices with their start and end apart: 9 -> 3, of which waited for: 5 -> 3; matrix products, arithmetic and copies ran while one was open for 7% -> 0% of each run, Pallas kernels for 0% -> 21%
where the time goes in v1:
time: 249 us
  waiting for transfers between devices  101 us (41%)
  Pallas kernels  64.7 us (26%)
  blocking collectives  60.5 us (24%)
  starting transfers between devices  11.4 us (5%)
  local copies, waits for them, and re-layouts  6.39 us (3%)
  other arithmetic  3.79 us (2%)
    all_to_all x3, waiting for transfers between devices, exchange(): lax.all_to_all(shaped, AXES, split_axis=0, concat_axis=0, tiled=True)  101 us
    all_to_all x1, blocking collectives, exchange(): lax.all_to_all(shaped, AXES, split_axis=0, concat_axis=0, tiled=True)  60.5 us
    pallas_call x2, Pallas kernels, shards(): pl.pallas_call(functools.partial(slots_kernel, slots, first), out_shape=[...  36.4 us
    pallas_call x1, Pallas kernels, shards(): pl.pallas_call(functools.partial(head_kernel, chunks, slots), out_shape=j...  16.2 us
    all_to_all x3, starting transfers between devices, exchange(): lax.all_to_all(shaped, AXES, split_axis=0, concat_axis=0, tiled=True)  11.4 us
    pallas_call x1, Pallas kernels, shards(): pl.pallas_call(functools.partial(combine_kernel, chunks, per), out_shape=...  6.1 us
    pallas_call x1, Pallas kernels, shards(): pl.pallas_call(functools.partial(dispatch_kernel, chunks, per), out_shape...  5.94 us
  transfers between devices with their start and end apart: 3, of which 3 were waited for; matrix products, arithmetic and copies ran while one was open for 0% of the time, Pallas kernels for 21%

profile of v1, /device:TPU:0, one launch (start us, length us, event | category | flops | bytes accessed | tf_op | source)
XLA Modules:
  0.0 248.6 jit_solution(8161079741910321172)
XLA Ops:
  0.7 0.7 add_select_fusion.1
  1.3 1.5 copy.16.owner_col
  2.8 1.5 copy.15.lang_col
  4.4 1.6 select_convert_fusion.meta
  6.0 5.9 %shard_map.94 = (s32[1,512]{1,0:T(1,128)}, bf16[512,2176]{1,0:T(8,128)(2,1)}, bf16[512,2176]{1,0:T(8,128)(2,1)}) custom-call(s32[512,1]{1,0:T(8,128)} %copy.15.lang_col, s32[1,512]{1,0:T(1,128)} %bitcast.18, s32[256,1]{1,0:T(8,128)} %copy.16.owner_col, bf16[512,2048]{1,0:T(8,128)(2,1)} %hidden.1, bf16[512,128]{1,0:T(8,128)(2,1)} %select_convert_fusion.meta), custom_call_target="tpu_custom_call" | custom-call | flops 2281701376 | bytes 8388608 | tf_op jit(solution)/shard_map/pallas_call | solution.py:177
  11.9 60.5 %all_to_all.20 = bf16[32,16,2176]{2,1,0:T(8,128)(2,1)} all-to-all(bf16[32,16,2176]{2,1,0:T(8,128)(2,1)} %bitcast.16), channel_id=1, replica_groups=mesh['vocab'=8,'fsdp'=4] {'vocab','fsdp'}, dimensions={0} | all-to-all | bytes 4456448 | tf_op jit(solution)/shard_map/all_to_all | solution.py:194
  72.4 0.0 copy-start.3
  72.4 0.0 copy-start.2
  72.4 2.9 %all-to-all-start = ((bf16[32,16,2176]{2,1,0:T(8,128)(2,1)}), bf16[32,16,2176]{2,1,0:T(8,128)(2,1)S(1)}, u32[]{:S(2)}, u32[]{:S(2)}) async-start(bf16[32,16,2176]{2,1,0:T(8,128)(2,1)} %bitcast.12), calls=%async_computation | async-start | bytes 4456448 | tf_op jit(solution)/shard_map/all_to_all | solution.py:194
  75.4 0.0 copy-done.3
  75.4 0.1 compare_convert_fusion
  75.4 0.0 copy-done.2
  75.4 0.2 multiply_reduce_fusion
  75.6 0.1 copy.17
  75.7 0.6 reshape.100.blocks
  76.3 18.2 %shard_map.96 = (bf16[512,2176]{1,0:T(8,128)(2,1)}, bf16[512,2048]{1,0:T(8,128)(2,1)}, bf16[512,1024]{1,0:T(8,128)(2,1)}) custom-call(s32[48]{0:T(128)} %reshape.100.blocks, bf16[512,2176]{1,0:T(8,128)(2,1)} %bitcast.11, bf16[8192,2048]{1,0:T(8,128)(2,1)} %slab.3), custom_call_target="tpu_custom_call" | custom-call | flops 4294967296 | bytes 29360128 | tf_op jit(solution)/shard_map/pallas_call | solution.py:202
  94.5 32.4 %all-to-all-done = bf16[32,16,2176]{2,1,0:T(8,128)(2,1)S(1)} async-done(((bf16[32,16,2176]{2,1,0:T(8,128)(2,1)}), bf16[32,16,2176]{2,1,0:T(8,128)(2,1)S(1)}, u32[]{:S(2)}, u32[]{:S(2)}) %all-to-all-start) | async-done | bytes 2228256 | tf_op jit(solution)/shard_map/all_to_all | solution.py:194
  127.0 0.0 copy-start
  127.0 1.4 copy-done
  128.3 4.2 %all-to-all-start.3 = ((bf16[32,16,2176]{2,1,0:T(8,128)(2,1)}), bf16[32,16,2176]{2,1,0:T(8,128)(2,1)}, u32[]{:S(2)}, u32[]{:S(2)}) async-start(bf16[32,16,2176]{2,1,0:T(8,128)(2,1)} %bitcast.14), calls=%async_computation.3 | async-start | bytes 4456448 | tf_op jit(solution)/shard_map/all_to_all | solution.py:194
  132.5 18.2 %shard_map.95 = (bf16[512,2176]{1,0:T(8,128)(2,1)}, bf16[512,2048]{1,0:T(8,128)(2,1)}, bf16[512,1024]{1,0:T(8,128)(2,1)}) custom-call(s32[48]{0:T(128)} %reshape.100.blocks, bf16[512,2176]{1,0:T(8,128)(2,1)} %bitcast.10, bf16[8192,2048]{1,0:T(8,128)(2,1)} %slab.3), custom_call_target="tpu_custom_call" | custom-call | flops 4294967296 | bytes 29360128 | tf_op jit(solution)/shard_map/pallas_call | solution.py:202
  150.7 33.4 %all-to-all-done.3 = bf16[32,16,2176]{2,1,0:T(8,128)(2,1)} async-done(((bf16[32,16,2176]{2,1,0:T(8,128)(2,1)}), bf16[32,16,2176]{2,1,0:T(8,128)(2,1)}, u32[]{:S(2)}, u32[]{:S(2)}) %all-to-all-start.3) | async-done | bytes 2228256 | tf_op jit(solution)/shard_map/all_to_all | solution.py:194
  184.1 4.4 %all-to-all-start.1 = ((bf16[32,16,2176]{2,1,0:T(8,128)(2,1)}), bf16[32,16,2176]{2,1,0:T(8,128)(2,1)S(1)}, u32[]{:S(2)}, u32[]{:S(2)}) async-start(bf16[32,16,2176]{2,1,0:T(8,128)(2,1)} %bitcast.15), calls=%async_computation.1 | async-start | bytes 4456448 | tf_op jit(solution)/shard_map/all_to_all | solution.py:194
  188.5 16.2 %shard_map.98 = bf16[8192,2048]{1,0:T(8,128)(2,1)} custom-call(bf16[512,2048]{1,0:T(8,128)(2,1)} %get-tuple-element.21.refs_0_, bf16[512,1024]{1,0:T(8,128)(2,1)} %get-tuple-element.22.refs_1_, bf16[512,2048]{1,0:T(8,128)(2,1)} %get-tuple-element.23.refs_2_, bf16[512,1024]{1,0:T(8,128)(2,1)} %get-tuple-element.24.refs_3_), custom_call_target="tpu_custom_call" | custom-call | flops 4294967296 | bytes 33554432 | tf_op jit(solution)/shard_map/pallas_call | solution.py:243
  204.7 35.3 %all-to-all-done.1 = bf16[32,16,2176]{2,1,0:T(8,128)(2,1)S(1)} async-done(((bf16[32,16,2176]{2,1,0:T(8,128)(2,1)}), bf16[32,16,2176]{2,1,0:T(8,128)(2,1)S(1)}, u32[]{:S(2)}, u32[]{:S(2)}) %all-to-all-start.1) | async-done | bytes 2228256 | tf_op jit(solution)/shard_map/all_to_all | solution.py:194
  239.9 0.0 copy-start.1
  239.9 1.3 copy-done.1
  241.3 6.1 %shard_map.97 = (bf16[512,2048]{1,0:T(8,128)(2,1)}, bf16[1,512]{1,0:T(2,128)(2,1)}) custom-call(s32[1,512]{1,0:T(1,128)} %get-tuple-element.14.place, bf16[512,2176]{1,0:T(8,128)(2,1)} %bitcast.13, bf16[512,2176]{1,0:T(8,128)(2,1)} %bitcast.9.refs_1_), custom_call_target="tpu_custom_call" | custom-call | flops 2281701376 | bytes 8388608 | tf_op jit(solution)/shard_map/pallas_call | solution.py:256
  247.4 1.2 reduce
  (3 shorter events, 0.0 us)
Async XLA Ops:
  72.4 2.9 %copy-start.3 = (s32[256]{0:T(256)S(1)}, s32[256]{0:T(256)}, u32[]{:S(2)}) copy-start(s32[256]{0:T(256)} %param.10) | copy-start | bytes 3076
  72.4 3.0 %copy-start.2 = (s32[256,6]{0,1:T(8,128)S(1)}, s32[256,6]{0,1:T(8,128)}, u32[]{:S(2)}) copy-start(s32[256,6]{0,1:T(8,128)} %param.9) | copy-start | bytes 18436
  72.4 54.5 %all-to-all-start = ((bf16[32,16,2176]{2,1,0:T(8,128)(2,1)}), bf16[32,16,2176]{2,1,0:T(8,128)(2,1)S(1)}, u32[]{:S(2)}, u32[]{:S(2)}) async-start(bf16[32,16,2176]{2,1,0:T(8,128)(2,1)} %bitcast.12), calls=%async_computation | async-start | bytes 4456448 | tf_op jit(solution)/shard_map/all_to_all | solution.py:194
  127.0 1.4 copy-start
  128.3 55.8 %all-to-all-start.3 = ((bf16[32,16,2176]{2,1,0:T(8,128)(2,1)}), bf16[32,16,2176]{2,1,0:T(8,128)(2,1)}, u32[]{:S(2)}, u32[]{:S(2)}) async-start(bf16[32,16,2176]{2,1,0:T(8,128)(2,1)} %bitcast.14), calls=%async_computation.3 | async-start | bytes 4456448 | tf_op jit(solution)/shard_map/all_to_all | solution.py:194
  184.1 55.8 %all-to-all-start.1 = ((bf16[32,16,2176]{2,1,0:T(8,128)(2,1)}), bf16[32,16,2176]{2,1,0:T(8,128)(2,1)S(1)}, u32[]{:S(2)}, u32[]{:S(2)}) async-start(bf16[32,16,2176]{2,1,0:T(8,128)(2,1)} %bitcast.15), calls=%async_computation.1 | async-start | bytes 4456448 | tf_op jit(solution)/shard_map/all_to_all | solution.py:194
  239.9 1.3 copy-start.1

commit v2 on v0

v2 whole, which is shorter than its diff:
```python
import functools

import jax
import jax.numpy as jnp
from jax import lax
from jax.experimental import pallas as pl
from jax.experimental.pallas import tpu as pltpu
from jax.sharding import PartitionSpec as P

BLOCK = 128
SB = 8
LB = 6
CAP = 4
SMOOTH = 0.1
AXES = ("vocab", "fsdp")
SIDE = 8
VMEM = 56 * 1024 * 1024
F32 = jnp.float32
BF16 = jnp.bfloat16


def one_hot(condition):
    return condition.astype(F32).astype(BF16)


def matmul(a, b, contract_a=1, contract_b=0):
    return lax.dot_general(
        a, b, (((contract_a,), (contract_b,)), ((), ())), preferred_element_type=F32
    )


def stack_rows(rows, width):
    line = lax.broadcasted_iota(jnp.int32, (SIDE, width), 0)
    total = jnp.zeros((SIDE, width), rows[0].dtype)
    for i, row in enumerate(rows):
        total = jnp.where(line == i, row, total)
    return total


def place_kernel(owned, lang_col, lang_row, owner_col, owner_row, label, weight, info, side):
    tokens = lang_row.shape[1]
    languages = owner_col.shape[0]
    slot_row = jnp.sum(
        jnp.where(
            lax.broadcasted_iota(jnp.int32, (languages, tokens), 0) == lang_row[...],
            owner_col[...],
            0,
        ),
        axis=0,
        keepdims=True,
    )
    slot_col = jnp.sum(
        jnp.where(
            lax.broadcasted_iota(jnp.int32, (tokens, languages), 1) == lang_col[...],
            owner_row[...],
            0,
        ),
        axis=1,
        keepdims=True,
    )
    before = lax.broadcasted_iota(jnp.int32, (tokens, tokens), 0) < lax.broadcasted_iota(
        jnp.int32, (tokens, tokens), 1
    )
    rank = jnp.sum(
        jnp.where((slot_col == slot_row) & before, 1, 0), axis=0, keepdims=True
    )
    dest = slot_row // owned
    position = jnp.sum(
        jnp.where((slot_col // owned == dest) & before, 1, 0), axis=0, keepdims=True
    )
    code = (slot_row - dest * owned) * CAP + rank + 1
    info[...] = stack_rows([dest, position], tokens)
    high = label[...] // BLOCK
    side[...] = stack_rows(
        [
            weight[...].astype(F32),
            high.astype(F32),
            (label[...] - high * BLOCK).astype(F32),
            code.astype(F32),
        ],
        tokens,
    ).astype(BF16)


def placing(info, capacity, rows):
    index = lax.broadcasted_iota(jnp.int32, (rows, 1), 0)
    return one_hot(index == info[0:1, :] * capacity + info[1:2, :])


def send_kernel(capacity, info, hidden, side, out_a, out_b, side_out):
    picks = placing(info, capacity, out_a.shape[0])
    split = out_a.shape[1]
    out_a[...] = matmul(picks, hidden[:, :split]).astype(BF16)
    out_b[...] = matmul(picks, hidden[:, split:]).astype(BF16)
    side_out[...] = matmul(side[...], picks, 1, 1)


def slot_picks(side, step, capacity, rows):
    buffer_rows = side.shape[1]
    index = lax.broadcasted_iota(jnp.int32, (rows, 1), 0)
    source = lax.broadcasted_iota(jnp.int32, (1, buffer_rows), 1) // capacity
    code = side[3:4, :].astype(jnp.int32) - 1
    where = jnp.where((code >= 0) & (code // CAP == step), source * CAP + code % CAP, -1)
    return one_hot(index == where)


def all_picks(side, owned, rows, capacity):
    buffer_rows = side.shape[1]
    index = lax.broadcasted_iota(jnp.int32, (owned * rows, 1), 0)
    source = lax.broadcasted_iota(jnp.int32, (1, buffer_rows), 1) // capacity
    code = side[3:4, :].astype(jnp.int32) - 1
    where = jnp.where(code >= 0, code // CAP * rows + source * CAP + code % CAP, -1)
    return one_hot(index == where)


def logits_kernel(capacity, side, incoming, slab, partial, rows_out):
    picks = slot_picks(side, pl.program_id(0), capacity, rows_out.shape[0])
    rows_out[...] = matmul(picks, incoming[...]).astype(BF16)
    partial[...] = matmul(rows_out[...], slab[...], 1, 1)


def loss_kernel(
    capacity, owned, blocks, side, incoming, slab, partial, rows_out, grads_out, back, loss_out, held
):
    step = pl.program_id(0)
    rows, columns = partial.shape
    picks = slot_picks(side, step, capacity, rows)
    rows_out[...] = matmul(picks, incoming[...]).astype(BF16)
    logits = partial[...] + matmul(rows_out[...], slab[...], 1, 1)
    extra = matmul(picks, side[...].astype(BF16), 1, 1)
    weights = extra[:, 0:1]
    targets = (extra[:, 1:2] * BLOCK + extra[:, 2:3]).astype(jnp.int32)
    column = lax.broadcasted_iota(jnp.int32, (1, columns), 1)
    listed = jnp.full((1, columns), -1, jnp.int32)
    for j in range(LB):
        named = blocks[step * LB + j]
        listed = jnp.where(column // BLOCK == named, j * BLOCK + column % BLOCK, listed)
    used = listed >= 0
    count = LB * BLOCK
    row_max = jnp.max(jnp.where(used, logits, -jnp.inf), axis=1, keepdims=True)
    shifted = jnp.where(used, logits - row_max, 0.0)
    powers = jnp.where(used, jnp.exp(shifted), 0.0)
    sums = jnp.sum(powers, axis=1, keepdims=True)
    log_sums = jnp.log(sums)
    is_target = listed == targets
    at_target = jnp.sum(jnp.where(is_target, shifted, 0.0), axis=1, keepdims=True) - log_sums
    all_of_them = jnp.sum(shifted, axis=1, keepdims=True) - count * log_sums
    losses = -(1.0 - SMOOTH) * at_target - SMOOTH / count * all_of_them
    grads = weights * (
        powers * (1.0 / sums) - jnp.where(is_target, 1.0 - SMOOTH, 0.0) - SMOOTH / count
    )
    grads = jnp.where(used, grads, 0.0).astype(BF16)
    grads_out[...] = grads
    here = pl.ds(pl.multiple_of(step * rows, rows), rows)
    held[here, :] = matmul(grads, slab[...]).astype(BF16)
    lane = lax.broadcasted_iota(jnp.int32, (rows, BLOCK), 1)
    tail = jnp.where(lane == 0, losses, 0.0).astype(BF16)
    line = matmul(tail, picks, 0, 0)[:SIDE, :]

    @pl.when(step == 0)
    def _():
        loss_out[...] = line

    @pl.when(step > 0)
    def _():
        loss_out[...] += line

    @pl.when(step == owned - 1)
    def _():
        back[...] = matmul(all_picks(side, owned, rows, capacity), held[...], 0, 0).astype(BF16)


def back_kernel(capacity, owned, side, grads, slab, back, held):
    step = pl.program_id(0)
    rows = grads.shape[0]
    here = pl.ds(pl.multiple_of(step * rows, rows), rows)
    held[here, :] = matmul(grads[...], slab[...]).astype(BF16)

    @pl.when(step == owned - 1)
    def _():
        back[...] = matmul(all_picks(side, owned, rows, capacity), held[...], 0, 0).astype(BF16)


def head_kernel(rows_a, rows_b, grads, out):
    split = rows_a.shape[1]
    out[:, :split] = matmul(grads[...], rows_a[...], 0, 0).astype(BF16)
    out[:, split:] = matmul(grads[...], rows_b[...], 0, 0).astype(BF16)


def combine_kernel(capacity, info, part_a, part_b, losses, hidden_out, loss_out):
    split = part_a.shape[1]
    picks = placing(info, capacity, part_a.shape[0])
    hidden_out[:, :split] = matmul(picks, part_a[...], 0, 0).astype(BF16)
    hidden_out[:, split:] = matmul(picks, part_b[...], 0, 0).astype(BF16)
    loss_out[...] = matmul(losses[...].astype(BF16), picks)[0:1, :].astype(BF16)


def exchanged(capacity, devices, info, side, hidden, head_weight, blocks):
    tokens, features = hidden.shape
    split = features // 4 * 3
    rest = features - split
    slab_rows = SB * BLOCK
    owned = head_weight.shape[0] // slab_rows
    rows = devices * CAP
    buffer_rows = devices * capacity
    places = owned * rows
    params = pltpu.CompilerParams(vmem_limit_bytes=VMEM)

    def shape(*dims, dtype=BF16):
        return jax.ShapeDtypeStruct(dims, dtype)

    def cost(macs, moved):
        return pl.CostEstimate(flops=2 * macs, bytes_accessed=moved, transcendentals=0)

    def whole(height, width):
        return pl.BlockSpec((height, width), lambda s, *_: (0, 0))

    def per_slot(height, width):
        return pl.BlockSpec((height, width), lambda s, *_: (s, 0))

    def exchange(values):
        shaped = values.reshape(devices, capacity, values.shape[1])
        return lax.all_to_all(shaped, AXES, split_axis=0, concat_axis=0, tiled=True).reshape(
            values.shape
        )

    def exchange_side(values):
        shaped = values.reshape(values.shape[0], devices, capacity)
        return lax.all_to_all(shaped, AXES, split_axis=1, concat_axis=1, tiled=True).reshape(
            values.shape
        )

    slab_a = per_slot(slab_rows, split)
    slab_b = pl.BlockSpec((slab_rows, rest), lambda s, *_: (s, split // rest))
    out_a, out_b, side_out = pl.pallas_call(
        functools.partial(send_kernel, capacity),
        out_shape=[
            shape(buffer_rows, split),
            shape(buffer_rows, rest),
            shape(SIDE, buffer_rows, dtype=F32),
        ],
        compiler_params=params,
        cost_estimate=cost(buffer_rows * tokens * features, 8 << 20),
    )(info, hidden, side)
    in_side = exchange_side(side_out[:4])
    in_a = exchange(out_a)
    in_b = exchange(out_b)
    partial, rows_a = pl.pallas_call(
        functools.partial(logits_kernel, capacity),
        out_shape=[shape(places, slab_rows, dtype=F32), shape(places, split)],
        grid=(owned,),
        in_specs=[whole(4, buffer_rows), whole(buffer_rows, split), slab_a],
        out_specs=[per_slot(rows, slab_rows), per_slot(rows, split)],
        compiler_params=params,
        cost_estimate=cost(2 * places * slab_rows * split, 40 << 20),
    )(in_side, in_a, head_weight)
    rows_b, grads, back_b, losses = pl.pallas_call(
        functools.partial(loss_kernel, capacity, owned),
        out_shape=[
            shape(places, rest),
            shape(places, slab_rows),
            shape(buffer_rows, rest),
            shape(SIDE, buffer_rows, dtype=F32),
        ],
        grid_spec=pltpu.PrefetchScalarGridSpec(
            num_scalar_prefetch=1,
            grid=(owned,),
            in_specs=[
                whole(4, buffer_rows),
                whole(buffer_rows, rest),
                slab_b,
                per_slot(rows, slab_rows),
            ],
            out_specs=[
                per_slot(rows, rest),
                per_slot(rows, slab_rows),
                whole(buffer_rows, rest),
                whole(SIDE, buffer_rows),
            ],
            scratch_shapes=[pltpu.VMEM((places, rest), BF16)],
        ),
        compiler_params=params,
        cost_estimate=cost(2 * places * slab_rows * rest, 16 << 20),
    )(blocks, in_side, in_b, head_weight, partial)
    got_b = exchange(back_b)
    got_loss = exchange_side(losses[:1])
    back_a = pl.pallas_call(
        functools.partial(back_kernel, capacity, owned),
        out_shape=shape(buffer_rows, split),
        grid=(owned,),
        in_specs=[whole(4, buffer_rows), per_slot(rows, slab_rows), slab_a],
        out_specs=whole(buffer_rows, split),
        scratch_shapes=[pltpu.VMEM((places, split), BF16)],
        compiler_params=params,
        cost_estimate=cost(2 * places * slab_rows * split, 40 << 20),
    )(in_side, grads, head_weight)
    got_a = exchange(back_a)
    head_grad = pl.pallas_call(
        head_kernel,
        out_shape=shape(*head_weight.shape),
        grid=(owned,),
        in_specs=[per_slot(rows, split), per_slot(rows, rest), per_slot(rows, slab_rows)],
        out_specs=per_slot(slab_rows, features),
        compiler_params=params,
        cost_estimate=cost(places * slab_rows * features, 40 << 20),
    )(rows_a, rows_b, grads)
    hidden_grad, token_loss = pl.pallas_call(
        functools.partial(combine_kernel, capacity),
        out_shape=[shape(tokens, features), shape(1, tokens)],
        compiler_params=params,
        cost_estimate=cost(buffer_rows * tokens * features, 8 << 20),
    )(info, got_a, got_b, got_loss)
    return hidden_grad, token_loss.reshape(tokens), head_grad


def shards(
    hidden, head_weight, language_blocks, language_owner, token_language, labels, loss_weight
):
    devices = lax.axis_size("vocab") * lax.axis_size("fsdp")
    languages = language_owner.shape[0]
    tokens = hidden.shape[0]
    owned = languages // devices
    most = owned * CAP
    info, side = pl.pallas_call(
        functools.partial(place_kernel, owned),
        out_shape=[
            jax.ShapeDtypeStruct((SIDE, tokens), jnp.int32),
            jax.ShapeDtypeStruct((SIDE, tokens), BF16),
        ],
    )(
        token_language,
        token_language.reshape(1, tokens),
        language_owner[:, None],
        language_owner[None, :],
        labels[None, :],
        loss_weight[None, :],
    )
    self_index = lax.axis_index(AXES)
    own_slots = self_index * owned + jnp.arange(owned, dtype=jnp.int32)
    owns = (own_slots[:, None] == language_owner[None, :]).astype(jnp.int32)
    blocks = jnp.sum(owns[:, :, None] * language_blocks[None], axis=1).reshape(-1)
    values = (info, side, hidden, head_weight, blocks)
    full = functools.partial(exchanged, most, devices)
    if most % 32:
        return full(*values)
    packed = most // 4 * 3
    longest = lax.pmax(jnp.max(info[1]), AXES)
    return lax.cond(longest < packed, functools.partial(exchanged, packed, devices), full, *values)


def solution(mesh):
    in_specs = (
        P(AXES, None),
        P(AXES, None),
        P(),
        P(),
        P(AXES, None),
        P(AXES),
        P(AXES),
    )
    out_specs = (P(AXES, None), P(AXES), P(AXES, None))
    return jax.shard_map(shards, mesh=mesh, in_specs=in_specs, out_specs=out_specs, check_vma=False)
```

time: 768 us -> 271 us (0.35)
  waiting for transfers between devices: 274 us -> 42.4 us
  local copies, waits for them, and re-layouts: 191 us -> 10.9 us
  other arithmetic: 173 us -> 3.51 us
  blocking collectives: 13.6 us -> 125 us
  Pallas kernels: 0 us -> 78 us
  matrix products: 68.3 us -> 0 us
  starting transfers between devices: 39 us -> 8.79 us
    all_to_all x9 -> x3, waiting for transfers between devices: 274 us -> 42.4 us  [exchange(): lax.all_to_all(shaped, AXES, split_axis=0, concat_axis=0, tiled=True)]
    scatter-add x8 -> x0, other arithmetic: 106 us -> none  [slot_work(): jnp.zeros((SB, BLOCK, D), jnp.float32).at[blocks]]
    pallas_call x0 -> x7, Pallas kernels: none -> 78 us  [the longest x1 17.7 us: exchanged(): pl.pallas_call(functools.partial(logits_kernel, capacity), out_shape=[sha...]
    all_to_all x1 -> x3, blocking collectives: 13.6 us -> 82.6 us  [the longest x1 59.4 us: exchange(): lax.all_to_all(shaped, AXES, split_axis=0, concat_axis=0, tiled=True)]
    dot_general x24 -> x0, matrix products: 68.3 us -> none  [the longest x8 37.8 us: slot_work(): lax.dot_general(grads, token_rows, (((0,), (0,)), ((), ())), preferred_el...]
    dynamic_update_slice x8 -> x0, other arithmetic: 48.4 us -> none  [shards(): row_grads, losses, slab_grads = lax.map(one_slot, slot_inputs)]
    pmax x0 -> x1, blocking collectives: none -> 42.2 us  [shards(): longest = lax.pmax(jnp.max(info[1]), AXES)]
    squeeze x8 -> x0, local copies, waits for them, and re-layouts: 37.6 us -> none  [shards(): row_grads, losses, slab_grads = lax.map(one_slot, slot_inputs)]
  transfers between devices with their start and end apart: 9 -> 3, of which waited for: 5 -> 3; matrix products, arithmetic and copies ran while one was open for 7% -> 1% of each run, Pallas kernels for 0% -> 18%
where the time goes in v2:
time: 271 us; the launch traced here: 270 us
  blocking collectives  125 us (46%)
  Pallas kernels  78 us (29%)
  waiting for transfers between devices  42.4 us (16%)
  local copies, waits for them, and re-layouts  10.9 us (4%)
  starting transfers between devices  8.79 us (3%)
  other arithmetic  3.51 us (1%)
    all_to_all x1, blocking collectives, exchange(): lax.all_to_all(shaped, AXES, split_axis=0, concat_axis=0, tiled=True)  59.4 us
    all_to_all x3, waiting for transfers between devices, exchange(): lax.all_to_all(shaped, AXES, split_axis=0, concat_axis=0, tiled=True)  42.4 us
    pmax x1, blocking collectives, shards(): longest = lax.pmax(jnp.max(info[1]), AXES)  42.2 us
    all_to_all x2, blocking collectives, exchange_side(): lax.all_to_all(shaped, AXES, split_axis=1, concat_axis=1, tiled=True)  23.3 us
    pallas_call x1, Pallas kernels, exchanged(): pl.pallas_call(functools.partial(logits_kernel, capacity), out_shape=[sha...  17.7 us
    pallas_call x1, Pallas kernels, exchanged(): pl.pallas_call(functools.partial(loss_kernel, capacity, owned), out_shape...  16.8 us
    pallas_call x1, Pallas kernels, exchanged(): pl.pallas_call(head_kernel, out_shape=shape(*head_weight.shape), grid=(ow...  16.1 us
    pallas_call x1, Pallas kernels, exchanged(): pl.pallas_call(functools.partial(back_kernel, capacity, owned), out_shape...  16.1 us
  transfers between devices with their start and end apart: 3, of which 3 were waited for; matrix products, arithmetic and copies ran while one was open for 1% of the time, Pallas kernels for 18%

profile of v2, /device:TPU:0, one launch (start us, length us, event | category | flops | bytes accessed | tf_op | source)
XLA Modules:
  0.0 270.0 jit_solution(16053927411536979167)
XLA Ops:
  0.6 1.3 broadcast_in_dim.19.weight
  1.9 0.7 compare_convert_fusion
  2.7 1.5 copy.46.owner_col
  4.1 1.5 copy.45.lang_col
  5.7 1.6 shard_map.104
  7.3 0.6 slice_reduce_fusion.2
  7.9 42.2 %pmax.7 = s32[]{:T(128)} all-reduce(s32[]{:T(128)} %slice_reduce_fusion.2), channel_id=1, replica_groups=mesh['vocab'=8,'fsdp'=4] {'vocab','fsdp'}, use_global_device_ids=true, to_apply=%region_1.0 | all-reduce | flops 1 | bytes 8 | tf_op jit(solution)/shard_map/pmax | solution.py:347
  50.8 219.2 %conditional.1 = (bf16[512,2048]{1,0:T(8,128)(2,1)}, bf16[512]{0:T(512)(128)(2,1)}, bf16[8192,2048]{1,0:T(8,128)(2,1)}) conditional(s32[]{:T(128)} %convert_element_type.10, (s32[8,512]{1,0:T(8,128)S(1)}, bf16[512,2048]{1,0:T(8,128)(2,1)}, bf16[8,512]{1,0:T(8,128)(2,1)S(1)}, bf16[8192,2048]{1,0:T(8,128)(2,1)}, s32[8,256]{1,0:T(8,128)S(1)}, /*index=5*/(), ...), branch_computations={%region_3.0_spmd, %region_4.0_spmd} | conditional | flops 23622344704 | bytes 202753216 | solution.py:348
  51.0 4.7 %branch_1_fun.6 = (bf16[768,1536]{1,0:T(8,128)(2,1)}, bf16[768,512]{1,0:T(8,128)(2,1)}, f32[8,768]{1,0:T(8,128)}) custom-call(s32[8,512]{1,0:T(8,128)S(1)} %get-tuple-element.36.info, bf16[512,2048]{1,0:T(8,128)(2,1)} %get-tuple-element.68.hidden, bf16[8,512]{1,0:T(8,128)(2,1)S(1)} %get-tuple-element.38.side), custom_call_target="tpu_custom_call" | custom-call | flops 1610612736 | bytes 8388608 | tf_op jit(solution)/shard_map/cond/branch_1_fun/pallas_call | solution.py:235
  55.7 0.7 slice.12
  56.6 11.8 %all_to_all.51 = f32[4,32,24]{2,0,1:T(4,128)S(1)} all-to-all(f32[4,32,24]{2,0,1:T(4,128)S(1)} %copy.41), channel_id=1, replica_groups=mesh['vocab'=8,'fsdp'=4] {'vocab','fsdp'}, dimensions={1} | all-to-all | bytes 24576 | tf_op jit(solution)/shard_map/cond/branch_1_fun/all_to_all | solution.py:229
  68.4 59.4 %all_to_all.52 = bf16[32,24,1536]{2,1,0:T(8,128)(2,1)} all-to-all(bf16[32,24,1536]{2,1,0:T(8,128)(2,1)} %bitcast.37), channel_id=1, replica_groups=mesh['vocab'=8,'fsdp'=4] {'vocab','fsdp'}, dimensions={0} | all-to-all | bytes 4718592 | tf_op jit(solution)/shard_map/cond/branch_1_fun/all_to_all | solution.py:223
  127.8 2.6 all-to-all-start.1
  130.7 0.6 reshape.125.blocks
  131.3 0.7 reshape.108.side
  132.0 17.7 %branch_1_fun.7 = (f32[1024,1024]{1,0:T(8,128)}, bf16[1024,1536]{1,0:T(8,128)(2,1)}) custom-call(f32[4,768]{1,0:T(4,128)} %reshape.108.side, bf16[768,1536]{1,0:T(8,128)(2,1)} %bitcast.31, bf16[8192,2048]{1,0:T(8,128)(2,1)} %get-tuple-element.70.slab), custom_call_target="tpu_custom_call" | custom-call | flops 6442450944 | bytes 41943040 | tf_op jit(solution)/shard_map/cond/branch_1_fun/pallas_call | solution.py:248
  149.7 1.3 all-to-all-done.1
  151.0 0.9 copy-done.2
  151.9 16.8 %branch_1_fun.8 = (bf16[1024,512]{1,0:T(8,128)(2,1)}, bf16[1024,1024]{1,0:T(8,128)(2,1)}, bf16[768,512]{1,0:T(8,128)(2,1)}, f32[8,768]{1,0:T(8,128)}) custom-call(s32[48]{0:T(128)} %reshape.125.blocks, f32[4,768]{1,0:T(4,128)} %reshape.108.side, bf16[768,512]{1,0:T(8,128)(2,1)} %bitcast.35, bf16[8192,2048]{1,0:T(8,128)(2,1)} %get-tuple-element.70.slab, ...), custom_call_target="tpu_custom_call" | custom-call | flops 2147483648 | bytes 16777216 | tf_op jit(solution)/shard_map/cond/branch_1_fun/pallas_call | solution.py:257
  168.7 0.8 slice_reduce_fusion.1
  169.6 11.5 %all_to_all.53 = f32[1,32,24]{2,0,1:T(1,128)S(1)} all-to-all(f32[1,32,24]{2,0,1:T(1,128)S(1)} %bitcast.45), channel_id=1, replica_groups=mesh['vocab'=8,'fsdp'=4] {'vocab','fsdp'}, dimensions={1} | all-to-all | bytes 6144 | tf_op jit(solution)/shard_map/cond/branch_1_fun/all_to_all | solution.py:229
  181.0 2.6 all-to-all-start.4
  183.7 16.1 %branch_1_fun.9 = bf16[768,1536]{1,0:T(8,128)(2,1)} custom-call(f32[4,768]{1,0:T(4,128)} %reshape.108.side, bf16[1024,1024]{1,0:T(8,128)(2,1)} %get-tuple-element.45.grads, bf16[8192,2048]{1,0:T(8,128)(2,1)} %get-tuple-element.70.slab), custom_call_target="tpu_custom_call" | custom-call | flops 6442450944 | bytes 41943040 | tf_op jit(solution)/shard_map/cond/branch_1_fun/pallas_call | solution.py:287
  199.7 4.5 %all-to-all-done.4 = bf16[32,24,512]{2,1,0:T(8,128)(2,1)S(1)} async-done(((bf16[32,24,512]{2,1,0:T(8,128)(2,1)}), bf16[32,24,512]{2,1,0:T(8,128)(2,1)S(1)}, u32[]{:S(2)}, u32[]{:S(2)}) %all-to-all-start.4) | async-done | bytes 786464 | tf_op jit(solution)/shard_map/cond/branch_1_fun/all_to_all | solution.py:223
  204.3 3.5 %all-to-all-start.3 = ((bf16[32,24,1536]{2,1,0:T(8,128)(2,1)}), bf16[32,24,1536]{2,1,0:T(8,128)(2,1)S(1)}, u32[]{:S(2)}, u32[]{:S(2)}) async-start(bf16[32,24,1536]{2,1,0:T(8,128)(2,1)} %bitcast.30), calls=%async_computation.3 | async-start | bytes 4718592 | tf_op jit(solution)/shard_map/cond/branch_1_fun/all_to_all | solution.py:223
  207.8 16.1 %branch_1_fun.11 = bf16[8192,2048]{1,0:T(8,128)(2,1)} custom-call(bf16[1024,1536]{1,0:T(8,128)(2,1)} %get-tuple-element.50.rows_a, bf16[1024,512]{1,0:T(8,128)(2,1)} %get-tuple-element.51.rows_b, bf16[1024,1024]{1,0:T(8,128)(2,1)} %get-tuple-element.45.grads), custom_call_target="tpu_custom_call" | custom-call | flops 4294967296 | bytes 41943040 | tf_op jit(solution)/shard_map/cond/branch_1_fun/pallas_call | solution.py:298
  224.4 0.7 reduce.16
  225.1 0.7 reshape.118.losses
  225.8 36.5 %all-to-all-done.3 = bf16[32,24,1536]{2,1,0:T(8,128)(2,1)S(1)} async-done(((bf16[32,24,1536]{2,1,0:T(8,128)(2,1)}), bf16[32,24,1536]{2,1,0:T(8,128)(2,1)S(1)}, u32[]{:S(2)}, u32[]{:S(2)}) %all-to-all-start.3) | async-done | bytes 2359328 | tf_op jit(solution)/shard_map/cond/branch_1_fun/all_to_all | solution.py:223
  262.2 1.4 copy-done.3
  263.7 5.1 %branch_1_fun.10 = (bf16[512,2048]{1,0:T(8,128)(2,1)}, bf16[1,512]{1,0:T(2,128)(2,1)}) custom-call(s32[8,512]{1,0:T(8,128)S(1)} %get-tuple-element.36.info, bf16[768,1536]{1,0:T(8,128)(2,1)} %bitcast.36, bf16[768,512]{1,0:T(8,128)(2,1)} %bitcast.40, f32[1,768]{1,0:T(1,128)} %reshape.118.losses), custom_call_target="tpu_custom_call" | custom-call | flops 1610612736 | bytes 8388608 | tf_op jit(solution)/shard_map/cond/branch_1_fun/pallas_call | solution.py:307
  268.7 1.3 reduce.6
  (14 shorter events, 1.0 us)
Async XLA Ops:
  68.4 62.0 %copy-start.7 = (s32[256,6]{0,1:T(8,128)S(1)}, s32[256,6]{0,1:T(8,128)}, u32[]{:S(2)}) copy-start(s32[256,6]{0,1:T(8,128)} %get-tuple-element.86) | copy-start | bytes 18436 | tf_op jit(solution)/shard_map/cond
  127.8 23.2 %all-to-all-start.1 = ((bf16[32,24,512]{2,1,0:T(8,128)(2,1)}), bf16[32,24,512]{2,1,0:T(8,128)(2,1)S(1)}, u32[]{:S(2)}, u32[]{:S(2)}) async-start(bf16[32,24,512]{2,1,0:T(8,128)(2,1)} %bitcast.9), calls=%async_computation.1 | async-start | bytes 1572864 | tf_op jit(solution)/shard_map/cond/branch_1_fun/all_to_all | solution.py:223
  151.0 0.9 copy-start.2
  181.0 23.2 %all-to-all-start.4 = ((bf16[32,24,512]{2,1,0:T(8,128)(2,1)}), bf16[32,24,512]{2,1,0:T(8,128)(2,1)S(1)}, u32[]{:S(2)}, u32[]{:S(2)}) async-start(bf16[32,24,512]{2,1,0:T(8,128)(2,1)} %bitcast.41), calls=%async_computation.4 | async-start | bytes 1572864 | tf_op jit(solution)/shard_map/cond/branch_1_fun/all_to_all | solution.py:223
  204.3 19.6 %copy-start.5 = (bf16[32,24,512]{2,1,0:T(8,128)(2,1)}, bf16[32,24,512]{2,1,0:T(8,128)(2,1)S(1)}, u32[]{:S(2)}) copy-start(bf16[32,24,512]{2,1,0:T(8,128)(2,1)S(1)} %all-to-all-done.4) | copy-start | bytes 2359300 | tf_op jit(solution)/shard_map/cond
  204.3 58.0 %all-to-all-start.3 = ((bf16[32,24,1536]{2,1,0:T(8,128)(2,1)}), bf16[32,24,1536]{2,1,0:T(8,128)(2,1)S(1)}, u32[]{:S(2)}, u32[]{:S(2)}) async-start(bf16[32,24,1536]{2,1,0:T(8,128)(2,1)} %bitcast.30), calls=%async_computation.3 | async-start | bytes 4718592 | tf_op jit(solution)/shard_map/cond/branch_1_fun/all_to_all | solution.py:223
  262.2 1.4 copy-start.3
